TPU v7x, 512 devices: a whole 4x8x8 slice. The times are simulated.
512 devices in a mesh: chan: 128 (over y, x_lo, z), win: 4 (over x_hi, core).
Axes of the slice: x: 4 (x_hi: 2, x_lo: 2; x = x_hi * 2 + x_lo), y: 8, z: 8, core: 2. Of those that a mesh axis runs over, the one named last changes fastest.
Arguments:
- spectra: bfloat16 [4096, 16, 2, 4096], P('chan', 'win'), may hold values from -500 to 500
- pair_list: int32 [12288, 3], P('chan'), may hold values from 0 to 4095, as said below
- quality: int32 [4096], P('chan'), may hold values 0 or 1
Outputs:
- stacked: float32 [12288, 1024], P('chan', 'win')
Inputs may be any that keep to these rules, and one draw needn't show every extreme that they name: `pair_list`: row i belongs to channel block b = i // 96 (channels b * 32 to b * 32 + 31). Column 0 is a source channel of that block, column 1 a receiver channel at most 64 channels from the source, column 2 is 1 for a used pair and 0 otherwise. In every draw used pairs reach that distance on both sides in every block whose neighbours lie on the fibre.
All inputs are finite; a program needn't handle non-finite values. No bound on the sum of `quality` on one device may be relied on, other than what follows from the above.
Results may differ from a plain program's by a relative error of at most 0.015.
Values may be sent and summed in bfloat16 or wider, within the bound.
A program may use at most 64 MiB of HBM per device.

v0:
```python
import math

import jax
import jax.numpy as jnp
from jax import lax
from jax.sharding import PartitionSpec as P

NF = 4096
LAGS = 1024
WB = 64
HB = 2


tiny_level = 1e-06
freq_block = 256


def shifted(block, axis, distance):
    devices = range(lax.axis_size(axis))
    route = [(i - distance, i) for i in devices if i - distance in devices]
    return lax.ppermute(block, axis, route)


def whiten(spectra, quality):
    chan_count = spectra.shape[0]
    sub_count = spectra.shape[1]
    bin_count = spectra.shape[3]
    values = spectra.astype(jnp.float32)
    magnitude = jnp.sqrt(values[:, :, 0] * values[:, :, 0] + values[:, :, 1] * values[:, :, 1])
    band_level = magnitude.reshape(chan_count, sub_count, bin_count // WB, WB).mean(axis=-1)
    factor = quality.astype(jnp.float32)[:, None, None, None, None] / (
        band_level[:, :, None, :, None] + tiny_level
    )
    shaped = values.reshape(chan_count, sub_count, 2, bin_count // WB, WB) * factor
    return shaped.reshape(spectra.shape).astype(jnp.bfloat16)


def lag_tables(first_bin, bin_total):
    frequency = first_bin + jnp.arange(bin_total, dtype=jnp.int32)
    lag_index = jnp.arange(LAGS, dtype=jnp.int32) - LAGS // 2
    phase_index = jnp.mod(frequency[:, None] * lag_index[None, :], 2 * NF)
    radians = phase_index.astype(jnp.float32) * (math.pi / NF)
    table_scale = 1.0 / math.sqrt(NF)
    return (
        (jnp.cos(radians) * table_scale).astype(jnp.bfloat16),
        (jnp.sin(radians) * table_scale).astype(jnp.bfloat16),
    )


def cross_lags(src_rows, rcv_rows, in_use, cos_table, sin_table):
    source = src_rows.astype(jnp.float32)
    receiver = rcv_rows.astype(jnp.float32)
    src_re = source[:, :, 0]
    src_im = source[:, :, 1]
    rcv_re = receiver[:, :, 0]
    rcv_im = receiver[:, :, 1]
    real_part = (src_re * rcv_re + src_im * rcv_im) * in_use[:, None, None]
    imag_part = (src_im * rcv_re - src_re * rcv_im) * in_use[:, None, None]
    row_count = real_part.shape[0] * real_part.shape[1]
    real_rows = real_part.astype(jnp.bfloat16).reshape(row_count, real_part.shape[2])
    imag_rows = imag_part.astype(jnp.bfloat16).reshape(row_count, real_part.shape[2])
    return jnp.dot(real_rows, cos_table, preferred_element_type=jnp.float32) - jnp.dot(
        imag_rows, sin_table, preferred_element_type=jnp.float32
    )


def on_device(spectra, pair_list, quality):
    chan_count = spectra.shape[0]
    sub_count = spectra.shape[1]
    bin_count = spectra.shape[3]
    pair_count = pair_list.shape[0]
    block_index = lax.axis_index("chan")
    whitened = whiten(spectra, quality)
    src_local = pair_list[:, 0] - block_index * chan_count
    rel_index = pair_list[:, 1] - (block_index - HB) * chan_count
    in_use = pair_list[:, 2].astype(jnp.float32)
    bin_block = min(bin_count, freq_block)
    blocks_near = []
    for offset in range(-HB, HB + 1):
        if offset == 0:
            blocks_near.append(whitened)
        else:
            blocks_near.append(shifted(whitened, "chan", -offset))

    def assemble(first_bin):
        return jnp.concatenate(
            [
                lax.dynamic_slice_in_dim(neighbour, first_bin, bin_block, 3)
                for neighbour in blocks_near
            ],
            axis=0,
        )

    def add_block(bin_step, lag_sums):
        first_bin = bin_step * bin_block
        own_bins = lax.dynamic_slice_in_dim(whitened, first_bin, bin_block, 3)
        src_rows = jnp.take(own_bins, src_local, axis=0)
        rcv_rows = jnp.take(assemble(first_bin), rel_index, axis=0)
        cos_table, sin_table = lag_tables(first_bin, bin_block)
        return lag_sums + cross_lags(src_rows, rcv_rows, in_use, cos_table, sin_table)

    start_sums = jnp.zeros((pair_count * sub_count, LAGS), jnp.float32)
    lag_sums = lax.fori_loop(0, bin_count // bin_block, add_block, start_sums)
    local_stack = lag_sums.reshape(pair_count, sub_count, LAGS).sum(axis=1)
    stacked = lax.psum_scatter(
        local_stack.astype(jnp.bfloat16), "win", scatter_dimension=1, tiled=True
    ).astype(jnp.float32)
    return stacked * (1.0 / math.sqrt(sub_count * lax.axis_size("win")))


def solution(mesh):
    return jax.shard_map(
        on_device,
        mesh=mesh,
        in_specs=(P("chan", "win", None, None), P("chan", None), P("chan")),
        out_specs=P("chan", "win"),
        check_vma=False,
    )
```

profile of v0, /device:TPU:57, one launch (start us, length us, event | category | flops | bytes accessed | tf_op | source)
XLA Modules:
  0.0 578.2 jit_solution(4198486657845277834)
XLA Ops:
  7.2 3.6 convert_element_type.93
  10.8 11.5 %sqrt_reduce_fusion = f32[32,4,4096]{2,1,0:T(4,128)S(1)} fusion(f32[32,4,2,4096]{3,2,1,0:T(2,128)S(1)} %convert_element_type.93), kind=kLoop, calls=%fused_computation.58 | loop fusion | flops 1572864 | bytes 6291456 | tf_op jit(solution)/shard_map/sqrt | solution.py:29
  22.3 3.3 sqrt.12
  25.7 3.4 reduce_sum.18
  31.7 5.2 mul.223
  36.9 6.1 %multiply_convert_fusion.8 = bf16[32,4,2,4096]{3,2,1,0:T(2,128)(2,1)} fusion(f32[32,4,4096]{2,1,0:T(4,128)} %mul.223, bf16[32,4,2,4096]{3,2,1,0:T(2,128)(2,1)S(1)} %copy-done), kind=kLoop, calls=%fused_computation.54 | loop fusion | flops 3145728 | bytes 6291456 | tf_op jit(solution)/shard_map/convert_element_type | solution.py:35
  43.0 12.4 %collective-permute-start.3 = (bf16[32,4,2,4096]{3,2,1,0:T(2,128)(2,1)}, bf16[32,4,2,4096]{3,2,1,0:T(2,128)(2,1)}, u32[]{:S(2)}, u32[]{:S(2)}) collective-permute-start(bf16[32,4,2,4096]{3,2,1,0:T(2,128)(2,1)} %multiply_convert_fusion.8), channel_id=1, source_target_pairs={{8,0},{12,4},{16,8},{20,12},{24,16},{28,20},{32,24},{36,28},{40,32... | collective-permute-start | bytes 6291464 | tf_op jit(solution)/shard_map/ppermute | solution.py:21
  57.5 3.1 collective-permute-start.1
  63.5 81.3 %collective-permute-done.3 = bf16[32,4,2,4096]{3,2,1,0:T(2,128)(2,1)} collective-permute-done((bf16[32,4,2,4096]{3,2,1,0:T(2,128)(2,1)}, bf16[32,4,2,4096]{3,2,1,0:T(2,128)(2,1)}, u32[]{:S(2)}, u32[]{:S(2)}) %collective-permute-start.3) | collective-permute-done | bytes 2097184 | tf_op jit(solution)/shard_map/ppermute | solution.py:21
  144.8 44.9 %collective-permute-done.2 = bf16[32,4,2,4096]{3,2,1,0:T(2,128)(2,1)} collective-permute-done((bf16[32,4,2,4096]{3,2,1,0:T(2,128)(2,1)}, bf16[32,4,2,4096]{3,2,1,0:T(2,128)(2,1)}, u32[]{:S(2)}, u32[]{:S(2)}) %collective-permute-start.2) | collective-permute-done | bytes 2097184 | tf_op jit(solution)/shard_map/ppermute | solution.py:21
  192.3 333.8 %while.16 = (s32[]{:T(128)}, f32[384,1024]{1,0:T(8,128)S(1)}, s32[96]{0:T(128)S(1)}, bf16[32,4,2,4096]{3,2,1,0:T(2,128)(2,1)}, s32[96]{0:T(128)S(1)}, /*index=5*...) while((s32[]{:T(128)}, f32[384,1024]{1,0:T(8,128)S(1)}, ...), condition=%wide.region_2.0_spmd.clone, body=%wide.region_1.2_spmd.clone.sunk | while | flops 413995968 | bytes 16420061 | solution.py:103
  201.3 2.9 subtract_reduce_fusion.2
  204.5 4.2 fusion.32
  208.7 4.4 select_add_fusion.2
  225.4 4.2 fusion.32
  229.5 4.4 select_add_fusion.2
  246.2 4.2 fusion.32
  250.4 4.4 select_add_fusion.2
  267.1 4.2 fusion.32
  271.3 4.4 select_add_fusion.2
  288.0 4.2 fusion.32
  292.1 4.4 select_add_fusion.2
  305.6 2.9 subtract_reduce_fusion.2
  308.8 4.2 fusion.32
  313.0 4.4 select_add_fusion.2
  329.7 4.2 fusion.32
  333.9 4.4 select_add_fusion.2
  347.3 2.9 subtract_reduce_fusion.2
  350.6 4.2 fusion.32
  354.7 4.4 select_add_fusion.2
  371.4 4.2 fusion.32
  375.6 4.4 select_add_fusion.2
  392.3 4.2 fusion.32
  396.5 4.4 select_add_fusion.2
  413.2 4.2 fusion.32
  417.3 4.4 select_add_fusion.2
  434.0 4.2 fusion.32
  438.2 4.4 select_add_fusion.2
  451.7 2.9 subtract_reduce_fusion.2
  454.9 4.2 fusion.32
  459.1 4.4 select_add_fusion.2
  475.8 4.2 fusion.32
  479.9 4.4 select_add_fusion.2
  496.6 4.2 fusion.32
  500.8 4.4 select_add_fusion.2
  517.5 4.2 fusion.32
  521.7 4.4 select_add_fusion.2
  528.4 41.5 %reduce-scatter.2.cloned.1.call-done = bf16[96,256]{1,0:T(8,128)(2,1)} async-done(((bf16[96,1024]{1,0:T(8,128)(2,1)}), bf16[96,256]{1,0:T(8,128)(2,1)}) %reduce-scatter.2.cloned.1.call-update) | async-done | bytes 49168 | tf_op jit(solution)/shard_map/reduce_scatter | solution.py:105
  (334 shorter events, 196.5 us)
Async XLA Ops:
  6.5 563.4 %reduce-scatter.2.cloned.1.call-start = ((), (), s32[]{:S(2)}) async-start(), calls=%async_computation.1 | async-start | bytes 245760 | tf_op jit(solution)/shard_map/reduce_scatter | solution.py:105
  31.7 5.2 copy-start
  36.9 26.6 %copy-start.1 = (s32[96,3]{0,1:T(4,128)S(1)}, s32[96,3]{0,1:T(4,128)}, u32[]{:S(2)}) copy-start(s32[96,3]{0,1:T(4,128)} %param.6) | copy-start | bytes 3460
  43.0 101.8 %collective-permute-start.3 = (bf16[32,4,2,4096]{3,2,1,0:T(2,128)(2,1)}, bf16[32,4,2,4096]{3,2,1,0:T(2,128)(2,1)}, u32[]{:S(2)}, u32[]{:S(2)}) collective-permute-start(bf16[32,4,2,4096]{3,2,1,0:T(2,128)(2,1)} %multiply_convert_fusion.8), channel_id=1, source_target_pairs={{8,0},{12,4},{16,8},{20,12},{24,16},{28,20},{32,24},{36,28},{40,32... | collective-permute-start | bytes 6291464 | tf_op jit(solution)/shard_map/ppermute | solution.py:21
  55.3 134.4 %collective-permute-start.2 = (bf16[32,4,2,4096]{3,2,1,0:T(2,128)(2,1)}, bf16[32,4,2,4096]{3,2,1,0:T(2,128)(2,1)}, u32[]{:S(2)}, u32[]{:S(2)}) collective-permute-start(bf16[32,4,2,4096]{3,2,1,0:T(2,128)(2,1)} %multiply_convert_fusion.8), channel_id=1, source_target_pairs={{4,0},{8,4},{12,8},{16,12},{20,16},{24,20},{28,24},{32,28},{36,32}... | collective-permute-start | bytes 6291464 | tf_op jit(solution)/shard_map/ppermute | solution.py:21
  57.5 132.2 %collective-permute-start.1 = (bf16[32,4,2,4096]{3,2,1,0:T(2,128)(2,1)}, bf16[32,4,2,4096]{3,2,1,0:T(2,128)(2,1)}, u32[]{:S(2)}, u32[]{:S(2)}) collective-permute-start(bf16[32,4,2,4096]{3,2,1,0:T(2,128)(2,1)} %multiply_convert_fusion.8), channel_id=1, source_target_pairs={{0,4},{4,8},{8,12},{12,16},{16,20},{20,24},{24,28},{28,32},{32,36}... | collective-permute-start | bytes 6291464 | tf_op jit(solution)/shard_map/ppermute | solution.py:21
  60.6 131.7 %collective-permute-start = (bf16[32,4,2,4096]{3,2,1,0:T(2,128)(2,1)}, bf16[32,4,2,4096]{3,2,1,0:T(2,128)(2,1)}, u32[]{:S(2)}, u32[]{:S(2)}) collective-permute-start(bf16[32,4,2,4096]{3,2,1,0:T(2,128)(2,1)} %multiply_convert_fusion.8), channel_id=1, source_target_pairs={{0,8},{4,12},{8,16},{12,20},{16,24},{20,28},{24,32},{28,36},{32,40... | collective-permute-start | bytes 6291464 | tf_op jit(solution)/shard_map/ppermute | solution.py:21
Sparse Core Ops, SparseCore 0:
  528.5 41.3 reduce-scatter.1
where the time goes:
time: 581 us; the launch traced here: 578 us
  waiting for transfers between devices  170 us (29%)
  local copies, waits for them, and re-layouts  144 us (25%)
  matrix products  138 us (24%)
  other arithmetic  89.5 us (15%)
  starting transfers between devices  20.5 us (4%)
  between operations  13.5 us (2%)
    ppermute x4, waiting for transfers between devices, shifted(): return lax.ppermute(block, axis, route)  129 us
    dot_general x16, matrix products, cross_lags(): jnp.dot(imag_rows, sin_table, preferred_element_type=jnp.float32)  71.2 us
    dot_general x16, matrix products, cross_lags(): jnp.dot(real_rows, cos_table, preferred_element_type=jnp.float32)  66.9 us
    while x64, local copies, waits for them, and re-layouts  65.7 us
    sub x16, other arithmetic, cross_lags(): imag_part = (src_im * rcv_re - src_re * rcv_im) * in_use[:, None, None]  46.9 us
    reduce_scatter x1, waiting for transfers between devices, on_device(): lax.psum_scatter(local_stack.astype(jnp.bfloat16), 'win', scatter_dimensi...  41.5 us
    gather x16, local copies, waits for them, and re-layouts, add_block(): rcv_rows = jnp.take(assemble(first_bin), rel_index, axis=0)  21.8 us
    gather x16, local copies, waits for them, and re-layouts, add_block(): src_rows = jnp.take(own_bins, src_local, axis=0)  21.7 us
  transfers between devices with their start and end apart: 5, of which 4 were waited for; matrix products, arithmetic and copies ran while one was open for 0% of the time, Pallas kernels for 0%

commit v1 on v0

v1 whole, which is shorter than its diff:
```python
import functools
import math

import jax
import jax.numpy as jnp
import numpy as np
import ml_dtypes
from jax import lax
from jax.experimental import pallas as pl
from jax.experimental.pallas import tpu as pltpu
from jax.sharding import PartitionSpec as P

MESH = pl.DeviceIdType.MESH
NF = 4096
LAGS = 1024
WB = 64
LANES = 128
tiny_level = 1e-06

RUNS = 8
PART = RUNS * LANES
PARTS = NF // PART


def lag_tables(groups):
    frequency = np.arange(NF, dtype=np.int64)
    lag_index = np.arange(LAGS, dtype=np.int64) - LAGS // 2
    phase = np.mod(frequency[:, None] * lag_index[None, :], 2 * NF)
    angle = np.arange(2 * NF, dtype=np.float64) * (math.pi / NF)
    scale = 1.0 / math.sqrt(NF)
    cos_of = (np.cos(angle) * scale).astype(ml_dtypes.bfloat16)
    sin_of = (-np.sin(angle) * scale).astype(ml_dtypes.bfloat16)
    both = np.stack([cos_of[phase], sin_of[phase]])
    both = both.reshape(2, PARTS, RUNS, LANES, groups, LAGS // groups)
    both = both.transpose(1, 4, 2, 0, 3, 5)
    return both.reshape(PARTS, groups, RUNS * 2 * LANES, LAGS // groups)


def band_mean():
    lane = np.arange(LANES)
    return ((lane[:, None] // WB == lane[None, :] // WB) / WB).astype(ml_dtypes.bfloat16)


def kernel(
    chan_total, quality, spectra, pairs, pairs_out, mean_of, table,
    out,
    near0, near1, near2, near3, loose, cross, sums, tab, pair_in, pair_near, src_at, rcv_at,
    core_out, core_in, home_out, home_in, half_out, half_in,
    part_send, part_recv, pair_send, pair_recv, pair_local, tab_sem, tail_send, tail_recv,
):
    near = (near0, near1, near2, near3)
    chan = lax.axis_index("chan")
    win = lax.axis_index("win")
    chans = spectra.shape[0]
    subs = spectra.shape[1]
    slots = pairs.shape[1]
    rows = 3 * slots
    wide = LAGS // 4
    core = lax.rem(win, 2)
    x_hi = win // 2
    right = (lax.rem(chan + 1, chan_total), win)
    left = (lax.rem(chan + chan_total - 1, chan_total), win)
    mate = (chan, win + 1 - 2 * core)
    across = (chan, lax.rem(win + 2, 4))

    tables = []
    for part in range(PARTS):
        for g in range(4):
            group = (g % 2) * 2 + (1 - core if g < 2 else core)
            copy = pltpu.make_async_copy(table.at[part, group], tab.at[part, g], tab_sem.at[part, g])
            copy.start()
            tables.append(copy)

    barrier = pltpu.get_barrier_semaphore()
    for peer in (left, right, mate, across):
        pl.semaphore_signal(barrier, inc=1, device_id=peer, device_id_type=MESH)
    pl.semaphore_wait(barrier, 4)

    pair_copies = []
    for side, peer in ((0, right), (1, left)):
        copy = pltpu.make_async_remote_copy(
            src_ref=pairs_out, dst_ref=pair_in.at[side],
            send_sem=pair_send.at[side], recv_sem=pair_recv.at[side],
            device_id=peer, device_id_type=MESH,
        )
        copy.start()
        pair_copies.append(copy)

    def whiten(part):
        step = 4

        def some(i, carry):
            first = i * step
            block = spectra[pl.ds(first, step), :, pl.ds(part * 2 * RUNS, 2 * RUNS), :]
            count = step * subs * RUNS
            loose[...] = block.astype(jnp.float32).reshape(2 * count, LANES)
            real = loose[pl.ds(0, count, stride=2), :]
            imag = loose[pl.ds(1, count, stride=2), :]
            magnitude = jnp.sqrt(real * real + imag * imag)
            level = jnp.dot(magnitude.astype(jnp.bfloat16), mean_of[...], preferred_element_type=jnp.float32)
            weight = 1.0 / (level + tiny_level)
            real = (real * weight).reshape(step, subs * RUNS, LANES)
            imag = (imag * weight).reshape(step, subs * RUNS, LANES)
            for j in range(step):
                good = quality[first + j].astype(jnp.float32)
                near[part][chans + first + j, 0 : subs * RUNS, :] = (real[j] * good).astype(jnp.bfloat16)
                near[part][chans + first + j, subs * RUNS :, :] = (imag[j] * good).astype(jnp.bfloat16)
            return carry

        lax.fori_loop(0, chans // step, some, 0)
        near[part][3 * chans] = jnp.zeros(near[part].shape[1:], jnp.bfloat16)

    part_copies = []
    for part in range(PARTS):
        whiten(part)
        copies = []
        for side, peer in ((0, right), (1, left)):
            copy = pltpu.make_async_remote_copy(
                src_ref=near[part].at[pl.ds(chans, chans)],
                dst_ref=near[part].at[pl.ds(2 * chans * side, chans)],
                send_sem=part_send.at[part, side], recv_sem=part_recv.at[part, side],
                device_id=peer, device_id_type=MESH,
            )
            copy.start()
            copies.append(copy)
        part_copies.append(copies)

    for copy in pair_copies:
        copy.wait()
    local = pltpu.make_async_copy(pair_in, pair_near, pair_local)
    local.start()
    local.wait()

    empty = 3 * chans
    base = (chan - 1) * chans

    def place(p, carry):
        def put(row, source, receiver, used, low, high):
            at = receiver - base
            fits = (used != 0) & (at >= low) & (at < high)
            src_at[row] = jnp.where(fits, source - base, empty)
            rcv_at[row] = jnp.where(fits, at, empty)

        put(p, pairs[0, p], pairs[1, p], pairs[2, p], 0, 3 * chans)
        has_left = (chan > 0).astype(jnp.int32)
        has_right = (chan < chan_total - 1).astype(jnp.int32)
        put(
            slots + p, pair_near[0, 0, p], pair_near[0, 1, p], pair_near[0, 2, p] * has_left,
            2 * chans, 2 * chans + chans * has_right,
        )
        put(
            2 * slots + p, pair_near[1, 0, p], pair_near[1, 1, p], pair_near[1, 2, p] * has_right,
            0, chans * has_left,
        )
        return carry

    lax.fori_loop(0, slots, place, 0)

    half = subs * RUNS

    def products(part):
        here = near[part]
        unroll = 4

        def some(i, carry):
            for j in range(unroll):
                p = i * unroll + j
                a = here[src_at[p]]
                b = here[rcv_at[p]]
                real = a[:half] * b[:half] + a[half:] * b[half:]
                imag = a[half:] * b[:half] - a[:half] * b[half:]
                real = real.astype(jnp.float32).reshape(subs, RUNS, LANES).sum(axis=0)
                imag = imag.astype(jnp.float32).reshape(subs, RUNS, LANES).sum(axis=0)
                cross[pl.ds(p, RUNS, stride=2 * rows), :] = real
                cross[pl.ds(p + rows, RUNS, stride=2 * rows), :] = imag
            return carry

        lax.fori_loop(0, rows // unroll, some, 0)

    def lags(part, g):
        wide_rows = jnp.concatenate(
            [cross[pl.ds(k * rows, rows), :].astype(jnp.bfloat16) for k in range(2 * RUNS)], axis=1
        )
        return jnp.dot(wide_rows, tab[part, g], preferred_element_type=jnp.float32)

    for copy in tables:
        copy.wait()

    def remote(src, dst, which, peer):
        copy = pltpu.make_async_remote_copy(
            src_ref=src, dst_ref=dst, send_sem=tail_send.at[which], recv_sem=tail_recv.at[which],
            device_id=peer, device_id_type=MESH,
        )
        copy.start()
        return copy

    tail = []
    for part in range(PARTS):
        for copy in part_copies[part]:
            copy.wait()
        products(part)
        for g in range(4):
            total = lags(part, g)
            if part > 0:
                total = total + sums[g]
            if part < PARTS - 1 or g >= 2:
                sums[g] = total
            else:
                core_out[g] = total.astype(jnp.bfloat16)
                tail.append(remote(core_out.at[g], core_in.at[g], g, mate))

    for g in range(2):
        tail[g].wait()
        both = sums[2 + g] + core_in[g].astype(jnp.float32)
        sums[2 + g] = both
        for side in range(2):
            home_out[side, g] = both[(1 + side) * slots : (2 + side) * slots].astype(jnp.bfloat16)
    back = [remote(home_out.at[0], home_in.at[1], 2, left), remote(home_out.at[1], home_in.at[0], 3, right)]
    for copy in back:
        copy.wait()

    def home_sum(g):
        return (
            sums[2 + g, 0:slots, :]
            + home_in[0, g].astype(jnp.float32)
            + home_in[1, g].astype(jnp.float32)
        )

    half_out[...] = home_sum(1 - x_hi).astype(jnp.bfloat16)
    last = remote(half_out, half_in, 4, across)
    mine = home_sum(x_hi)
    last.wait()
    out[...] = (mine + half_in[...].astype(jnp.float32)) * (1.0 / math.sqrt(subs * 4))


def on_device(chan_total, spectra, pair_list, quality):
    chans, subs = spectra.shape[0], spectra.shape[1]
    slots = pair_list.shape[0]
    rows = 3 * slots
    runs = NF // LANES
    tiles = spectra.reshape(chans, subs, 2, runs, LANES).transpose(0, 1, 3, 2, 4)
    tiles = tiles.reshape(chans, subs, 2 * runs, LANES)
    pairs = pair_list.T
    table = jnp.asarray(lag_tables(4))
    vmem = pl.BlockSpec(memory_space=pltpu.VMEM)
    smem = pl.BlockSpec(memory_space=pltpu.SMEM)
    wide = LAGS // 4
    near = pltpu.VMEM((3 * chans + 1, 2 * subs * RUNS, LANES), jnp.bfloat16)
    sem = pltpu.SemaphoreType.DMA
    return pl.pallas_call(
        functools.partial(kernel, chan_total),
        out_shape=jax.ShapeDtypeStruct((slots, wide), jnp.float32),
        in_specs=[smem, vmem, smem, vmem, vmem, pl.BlockSpec(memory_space=pl.ANY)],
        out_specs=vmem,
        scratch_shapes=[
            near, near, near, near,
            pltpu.VMEM((4 * subs * RUNS * 2, LANES), jnp.float32),
            pltpu.VMEM((2 * RUNS * rows, LANES), jnp.float32),
            pltpu.VMEM((4, rows, wide), jnp.float32),
            pltpu.VMEM((PARTS, 4, 2 * PART, wide), jnp.bfloat16),
            pltpu.VMEM((2,) + pairs.shape, jnp.int32),
            pltpu.SMEM((2,) + pairs.shape, jnp.int32),
            pltpu.SMEM((rows,), jnp.int32),
            pltpu.SMEM((rows,), jnp.int32),
            pltpu.VMEM((2, rows, wide), jnp.bfloat16),
            pltpu.VMEM((2, rows, wide), jnp.bfloat16),
            pltpu.VMEM((2, 2, slots, wide), jnp.bfloat16),
            pltpu.VMEM((2, 2, slots, wide), jnp.bfloat16),
            pltpu.VMEM((slots, wide), jnp.bfloat16),
            pltpu.VMEM((slots, wide), jnp.bfloat16),
            sem((PARTS, 2)), sem((PARTS, 2)), sem((2,)), sem((2,)), sem, sem((PARTS, 4)), sem((5,)), sem((5,)),
        ],
        compiler_params=pltpu.CompilerParams(
            collective_id=0, has_side_effects=True, vmem_limit_bytes=56 * 1024 * 1024
        ),
    )(quality, tiles, pairs, pairs, jnp.asarray(band_mean()), table)


def solution(mesh):
    return jax.shard_map(
        functools.partial(on_device, mesh.shape["chan"]),
        mesh=mesh,
        in_specs=(P("chan", "win", None, None), P("chan", None), P("chan")),
        out_specs=P("chan", "win"),
        check_vma=False,
    )
```

time: 581 us -> 84.3 us (0.15)
  the two profiles are of different devices: /device:TPU:57 before, /device:TPU:1 now
where the time goes in v1:
time: 84.3 us; the launch traced here: 84.2 us
  Pallas kernels  82.6 us (98%)
  local copies, waits for them, and re-layouts  1.54 us (2%)
    pallas_call x1, Pallas kernels, on_device(): pl.pallas_call(functools.partial(kernel, chan_total), out_shape=jax.Shape...  82.6 us

profile of v1, /device:TPU:1, one launch (start us, length us, event | category | flops | bytes accessed | tf_op | source)
XLA Modules:
  0.0 84.2 jit_solution(10433501792838510947)
XLA Ops:
  0.0 82.6 %shard_map.55 = f32[96,256]{1,0:T(8,128)} custom-call(s32[32]{0:T(128)} %quality.1, bf16[32,4,64,128]{3,2,1,0:T(8,128)(2,1)} %bitcast.6, s32[3,96]{1,0:T(4,128)} %bitcast.7, s32[3,96]{1,0:T(4,128)} %bitcast.8, bf16[128,128]{1,0:T(8,128)(2,1)} %constant.5.clone.mean_of, bf16[4,4,2048,256]{3,2,1,0:T(8,128)(2,1)} %constant.4.clone.table), custom_call_target="tpu_custom_call" | custom-call | tf_op jit(solution)/shard_map/pallas_call | solution.py:250
  82.6 1.5 %copy.8 = f32[96,256]{1,0:T(8,128)} copy(f32[96,256]{1,0:T(8,128)} %shard_map.55) | data formatting | bytes 196608

commit v2 on v1

v2 whole, which is shorter than its diff:
```python
import functools
import math

import jax
import jax.numpy as jnp
import numpy as np
import ml_dtypes
from jax import lax
from jax.experimental import pallas as pl
from jax.experimental.pallas import tpu as pltpu
from jax.sharding import PartitionSpec as P

MESH = pl.DeviceIdType.MESH
NF = 4096
LAGS = 1024
WB = 64
LANES = 128
tiny_level = 1e-06

RUNS = 8
GROUPS = NF // (RUNS * LANES)
PARTS = ((0, 0, 8), (1, 0, 8), (2, 0, 8), (3, 0, 4), (3, 4, 4))
WINS = 4
WIDE = LAGS // WINS


def lag_tables():
    frequency = np.arange(NF, dtype=np.int64)
    lag_index = np.arange(LAGS, dtype=np.int64) - LAGS // 2
    phase = np.mod(frequency[:, None] * lag_index[None, :], 2 * NF)
    angle = np.arange(2 * NF, dtype=np.float64) * (math.pi / NF)
    scale = 1.0 / math.sqrt(NF)
    cos_of = (np.cos(angle) * scale).astype(ml_dtypes.bfloat16)
    sin_of = (-np.sin(angle) * scale).astype(ml_dtypes.bfloat16)
    both = np.stack([cos_of[phase], sin_of[phase]])
    both = both.reshape(2, GROUPS, RUNS, LANES, WINS, WIDE)
    both = both.transpose(1, 4, 2, 0, 3, 5)
    return both.reshape(GROUPS, WINS, RUNS * 2 * LANES, WIDE)


def band_mean():
    lane = np.arange(LANES)
    return ((lane[:, None] // WB == lane[None, :] // WB) / WB).astype(ml_dtypes.bfloat16)


def kernel(
    chan_total, quality, pairs, pairs_out, mean_of, spectra, table,
    out,
    near0, near1, near2, near3, near4, fresh, loose, cross, left_rows, sums, tab,
    pair_in, pair_near, src_at, rcv_at,
    core_out, core_in, home_out, home_in, own_out, own_in,
    fresh_sem, tab_sem, part_send, part_recv, pair_send, pair_recv, pair_local, tail_send, tail_recv,
):
    near = (near0, near1, near2, near3, near4)
    chan = lax.axis_index("chan")
    win = lax.axis_index("win")
    chans = quality.shape[0]
    subs = spectra.shape[1]
    slots = pairs.shape[1]
    rows = 3 * slots
    core = lax.rem(win, 2)
    x_hi = win // 2
    has_left = (chan > 0).astype(jnp.int32)
    has_right = (chan < chan_total - 1).astype(jnp.int32)
    win_mate = x_hi * 2 + 1 - core
    win_across = (1 - x_hi) * 2 + core
    win_cross = (1 - x_hi) * 2 + 1 - core

    barrier = pltpu.get_barrier_semaphore()

    def greet(peer):
        pl.semaphore_signal(barrier, inc=1, device_id=peer, device_id_type=MESH)

    @pl.when(chan > 0)
    def _():
        greet((chan - 1, win))
        greet((chan - 1, win_across))

    @pl.when(chan < chan_total - 1)
    def _():
        greet((chan + 1, win))
        greet((chan + 1, win_across))

    greet((chan, win_mate))
    greet((chan, win_across))
    greet((chan, win_cross))

    fetched = []
    for group in range(GROUPS):
        copy = pltpu.make_async_copy(
            spectra.at[:, :, pl.ds(group * 2 * RUNS, 2 * RUNS), :], fresh.at[group], fresh_sem.at[group]
        )
        copy.start()
        fetched.append(copy)
    @pl.when(chan == 0)
    def _():
        for part in range(len(PARTS)):
            near[part][0:chans] = jnp.zeros((chans,) + near[part].shape[1:], jnp.bfloat16)
        pair_in[0] = jnp.zeros(pair_in.shape[1:], jnp.int32)
        home_in[0] = jnp.zeros(home_in.shape[1:], jnp.bfloat16)

    @pl.when(chan == chan_total - 1)
    def _():
        for part in range(len(PARTS)):
            near[part][2 * chans : 3 * chans] = jnp.zeros((chans,) + near[part].shape[1:], jnp.bfloat16)
        pair_in[1] = jnp.zeros(pair_in.shape[1:], jnp.int32)
        home_in[1] = jnp.zeros(home_in.shape[1:], jnp.bfloat16)

    def whiten(group):
        step = 4
        mine = [(p, first, runs) for p, (g, first, runs) in enumerate(PARTS) if g == group]
        fetched[group].wait()

        def some(i, carry):
            start = i * step
            block = fresh[group, pl.ds(start, step)]
            count = step * subs * RUNS
            loose[...] = block.astype(jnp.float32).reshape(2 * count, LANES)
            real = loose[pl.ds(0, count, stride=2), :]
            imag = loose[pl.ds(1, count, stride=2), :]
            magnitude = jnp.sqrt(real * real + imag * imag)
            level = jnp.dot(magnitude.astype(jnp.bfloat16), mean_of[...], preferred_element_type=jnp.float32)
            weight = 1.0 / (level + tiny_level)
            real = (real * weight).reshape(step, subs, RUNS, LANES)
            imag = (imag * weight).reshape(step, subs, RUNS, LANES)
            for j in range(step):
                good = quality[start + j].astype(jnp.float32)
                for p, first, runs in mine:
                    half = subs * runs
                    for k, values in ((0, real), (1, imag)):
                        kept = (values[j, :, first : first + runs] * good).reshape(half, LANES)
                        near[p][chans + start + j, k * half : (k + 1) * half, :] = kept.astype(jnp.bfloat16)
            return carry

        lax.fori_loop(0, chans // step, some, 0)
        for p, first, runs in mine:
            near[p][3 * chans] = jnp.zeros(near[p].shape[1:], jnp.bfloat16)

    def both_ways(to_right, to_left):
        @pl.when(chan < chan_total - 1)
        def _():
            to_right.start()

        @pl.when(chan > 0)
        def _():
            to_left.start()

    def both_waits(to_right, to_left):
        @pl.when(chan < chan_total - 1)
        def _():
            to_right.wait_send()
            to_left.wait_recv()

        @pl.when(chan > 0)
        def _():
            to_left.wait_send()
            to_right.wait_recv()

    def beside(src, dsts, send, recv):
        return [
            pltpu.make_async_remote_copy(
                src_ref=src, dst_ref=dsts[side], send_sem=send.at[side], recv_sem=recv.at[side],
                device_id=(peer, win), device_id_type=MESH,
            )
            for side, peer in ((0, chan + 1), (1, chan - 1))
        ]

    whiten(0)
    pl.semaphore_wait(barrier, 3 + 2 * has_left + 2 * has_right)

    pair_copies = beside(pairs_out, [pair_in.at[0], pair_in.at[1]], pair_send, pair_recv)
    part_copies = []
    for group in range(GROUPS):
        if group > 0:
            whiten(group)
        for p, (g, first, runs) in enumerate(PARTS):
            if g == group:
                copies = beside(
                    near[p].at[pl.ds(chans, chans)],
                    [near[p].at[pl.ds(0, chans)], near[p].at[pl.ds(2 * chans, chans)]],
                    part_send.at[p], part_recv.at[p],
                )
                both_ways(*copies)
                part_copies.append(copies)
        if group == 0:
            both_ways(*pair_copies)

    tables = []
    for group in range(GROUPS):
        for g, quarter in enumerate((win_cross, win_mate, win_across, win)):
            copy = pltpu.make_async_copy(table.at[group, quarter], tab.at[group, g], tab_sem.at[group, g])
            copy.start()
            tables.append(copy)

    both_waits(*pair_copies)
    local = pltpu.make_async_copy(pair_in, pair_near, pair_local)
    local.start()
    local.wait()

    empty = 3 * chans
    base = (chan - 1) * chans

    def place(p, carry):
        def put(row, source, receiver, used, low, high):
            at = receiver - base
            fits = (used != 0) & (at >= low) & (at < high)
            src_at[row] = jnp.where(fits, source - base, empty)
            rcv_at[row] = jnp.where(fits, at, empty)

        put(p, pairs[0, p], pairs[1, p], pairs[2, p], 0, 3 * chans)
        between = has_left * has_right
        put(
            slots + p, pair_near[0, 0, p], pair_near[0, 1, p], pair_near[0, 2, p] * between,
            2 * chans, 3 * chans,
        )
        put(
            2 * slots + p, pair_near[1, 0, p], pair_near[1, 1, p], pair_near[1, 2, p] * between,
            0, chans,
        )
        return carry

    lax.fori_loop(0, slots, place, 0)

    def products(part, low, high):
        runs = PARTS[part][2]
        half = subs * runs
        here = near[part]
        unroll = 4

        def fold(values):
            values = values.astype(jnp.float32).reshape(half // 8, 8, LANES).sum(axis=0)
            if runs == 4:
                values = values[:4] + values[4:]
            return values

        def some(i, carry):
            for j in range(unroll):
                p = low + i * unroll + j
                a = here[src_at[p]]
                b = here[rcv_at[p]]
                real = a[:half] * b[:half] + a[half:] * b[half:]
                imag = a[half:] * b[:half] - a[:half] * b[half:]
                cross[pl.ds(p, runs, stride=2 * rows), :] = fold(real)
                cross[pl.ds(p + rows, runs, stride=2 * rows), :] = fold(imag)
            return carry

        lax.fori_loop(0, (high - low) // unroll, some, 0)
        for k in range(2 * runs):
            left_rows[low:high, k * LANES : (k + 1) * LANES] = cross[k * rows + low : k * rows + high, :].astype(
                jnp.bfloat16
            )

    def lags(part, low, high, g):
        group, first, runs = PARTS[part]
        depth = 2 * runs * LANES
        return jnp.dot(
            left_rows[low:high, :depth], tab[group, g, 2 * first * LANES : 2 * first * LANES + depth, :],
            preferred_element_type=jnp.float32,
        )

    for copy in tables:
        copy.wait()

    for part in range(len(PARTS) - 1):
        both_waits(*part_copies[part])
        products(part, 0, rows)
        for g in range(WINS):
            total = lags(part, 0, rows, g)
            sums[g] = total if part == 0 else total + sums[g]

    def remote(src, dst, which, peer):
        return pltpu.make_async_remote_copy(
            src_ref=src, dst_ref=dst, send_sem=tail_send.at[which], recv_sem=tail_recv.at[which],
            device_id=peer, device_id_type=MESH,
        )

    part = len(PARTS) - 1
    both_waits(*part_copies[part])
    products(part, slots, rows)
    core_copies = []
    for g in range(2):
        core_out[g] = (lags(part, slots, rows, g) + sums[g, slots:rows]).astype(jnp.bfloat16)
        copy = remote(core_out.at[g], core_in.at[g], g, (chan, win_mate))
        copy.start()
        core_copies.append(copy)
    home_copies = []
    ahead = [lags(part, slots, rows, 2 + g) + sums[2 + g, slots:rows] for g in range(2)]
    for g, to_win in ((0, win_across), (1, win)):
        core_copies[g].wait()
        home_out[g] = (ahead[g] + core_in[g].astype(jnp.float32)).astype(jnp.bfloat16)
        copies = [
            remote(home_out.at[g, pl.ds(slots, slots)], home_in.at[0, g], 2 + 2 * g, (chan + 1, to_win)),
            remote(home_out.at[g, pl.ds(0, slots)], home_in.at[1, g], 3 + 2 * g, (chan - 1, to_win)),
        ]
        both_ways(*copies)
        home_copies.append(copies)

    products(part, 0, slots)
    own_copies = []
    for g, to_win in ((0, win_cross), (1, win_mate), (2, win_across)):
        own_out[g] = (lags(part, 0, slots, g) + sums[g, 0:slots]).astype(jnp.bfloat16)
        copy = remote(own_out.at[g], own_in.at[g], 6 + g, (chan, to_win))
        copy.start()
        own_copies.append(copy)
    total = lags(part, 0, slots, 3) + sums[3, 0:slots]
    for copy in own_copies:
        copy.wait()
    for g in range(3):
        total = total + own_in[g].astype(jnp.float32)
    for copies in home_copies:
        both_waits(*copies)
    for g in range(2):
        total = total + home_in[0, g].astype(jnp.float32) + home_in[1, g].astype(jnp.float32)
    out[...] = total * (1.0 / math.sqrt(subs * WINS))


def on_device(chan_total, spectra, pair_list, quality):
    chans, subs = spectra.shape[0], spectra.shape[1]
    slots = pair_list.shape[0]
    rows = 3 * slots
    runs = NF // LANES
    tiles = spectra.reshape(chans, subs, 2, runs, LANES).transpose(0, 1, 3, 2, 4)
    tiles = tiles.reshape(chans, subs, 2 * runs, LANES)
    pairs = pair_list.T
    vmem = pl.BlockSpec(memory_space=pltpu.VMEM)
    smem = pl.BlockSpec(memory_space=pltpu.SMEM)
    anywhere = pl.BlockSpec(memory_space=pl.ANY)
    sem = pltpu.SemaphoreType.DMA
    bf16 = jnp.bfloat16
    return pl.pallas_call(
        functools.partial(kernel, chan_total),
        out_shape=jax.ShapeDtypeStruct((slots, WIDE), jnp.float32),
        in_specs=[smem, smem, vmem, vmem, anywhere, anywhere],
        out_specs=vmem,
        scratch_shapes=[pltpu.VMEM((3 * chans + 1, 2 * subs * part[2], LANES), bf16) for part in PARTS]
        + [
            pltpu.VMEM((GROUPS, chans, subs, 2 * RUNS, LANES), bf16),
            pltpu.VMEM((4 * subs * RUNS * 2, LANES), jnp.float32),
            pltpu.VMEM((2 * RUNS * rows, LANES), jnp.float32),
            pltpu.VMEM((rows, 2 * RUNS * LANES), bf16),
            pltpu.VMEM((WINS, rows, WIDE), jnp.float32),
            pltpu.VMEM((GROUPS, WINS, 2 * RUNS * LANES, WIDE), bf16),
            pltpu.VMEM((2,) + pairs.shape, jnp.int32),
            pltpu.SMEM((2,) + pairs.shape, jnp.int32),
            pltpu.SMEM((rows,), jnp.int32),
            pltpu.SMEM((rows,), jnp.int32),
            pltpu.VMEM((2, 2 * slots, WIDE), bf16),
            pltpu.VMEM((2, 2 * slots, WIDE), bf16),
            pltpu.VMEM((2, 2 * slots, WIDE), bf16),
            pltpu.VMEM((2, 2, slots, WIDE), bf16),
            pltpu.VMEM((3, slots, WIDE), bf16),
            pltpu.VMEM((3, slots, WIDE), bf16),
            sem((GROUPS,)), sem((GROUPS, WINS)), sem((len(PARTS), 2)), sem((len(PARTS), 2)),
            sem((2,)), sem((2,)), sem, sem((9,)), sem((9,)),
        ],
        compiler_params=pltpu.CompilerParams(
            collective_id=0, has_side_effects=True, vmem_limit_bytes=56 * 1024 * 1024
        ),
    )(quality, pairs, pairs, jnp.asarray(band_mean()), tiles, jnp.asarray(lag_tables()))


def solution(mesh):
    return jax.shard_map(
        functools.partial(on_device, mesh.shape["chan"]),
        mesh=mesh,
        in_specs=(P("chan", "win", None, None), P("chan", None), P("chan")),
        out_specs=P("chan", "win"),
        check_vma=False,
    )
```

time: 84.3 us -> 74 us (0.88)
  the two profiles are of different devices: /device:TPU:1 before, /device:TPU:57 now
where the time goes in v2:
time: 74 us; the launch traced here: 73.8 us
  Pallas kernels  72.3 us (98%)
  local copies, waits for them, and re-layouts  1.54 us (2%)
    pallas_call x1, Pallas kernels, on_device(): pl.pallas_call(functools.partial(kernel, chan_total), out_shape=jax.Shape...  72.3 us
    unnamed x1, local copies, waits for them, and re-layouts  1.54 us

profile of v2, /device:TPU:57, one launch (start us, length us, event | category | flops | bytes accessed | tf_op | source)
XLA Modules:
  0.0 73.8 jit_solution(17730131289456584484)
XLA Ops:
  0.0 72.3 %shard_map.55 = f32[96,256]{1,0:T(8,128)} custom-call(s32[32]{0:T(128)} %quality.1, s32[3,96]{1,0:T(4,128)} %bitcast.7, s32[3,96]{1,0:T(4,128)} %bitcast.8, bf16[128,128]{1,0:T(8,128)(2,1)} %constant.4.clone.mean_of, bf16[32,4,64,128]{3,2,1,0:T(8,128)(2,1)} %bitcast.6, bf16[4,4,2048,256]{3,2,1,0:T(8,128)(2,1)} %constant.5.clone.table), custom_call_target="tpu_custom_call" | custom-call | tf_op jit(solution)/shard_map/pallas_call | solution.py:330
  72.3 1.5 %copy.8 = f32[96,256]{1,0:T(8,128)} copy(f32[96,256]{1,0:T(8,128)} %shard_map.55) | data formatting | bytes 196608

commit v3 on v2

--- a/solution.py
+++ b/solution.py
@@ -39,25 +39,27 @@
 
 
 def band_mean():
-    lane = np.arange(LANES)
-    return ((lane[:, None] // WB == lane[None, :] // WB) / WB).astype(ml_dtypes.bfloat16)
+    here = lax.broadcasted_iota(jnp.int32, (LANES, LANES), 0) // WB
+    there = lax.broadcasted_iota(jnp.int32, (LANES, LANES), 1) // WB
+    return jnp.where(here == there, 1.0 / WB, 0.0).astype(jnp.bfloat16)
 
 
 def kernel(
-    chan_total, quality, pairs, pairs_out, mean_of, spectra, table,
+    chan_total, quality_in, pairs_out, spectra, table,
     out,
     near0, near1, near2, near3, near4, fresh, loose, cross, left_rows, sums, tab,
-    pair_in, pair_near, src_at, rcv_at,
+    quality, pairs, pair_in, pair_near, src_at, rcv_at,
     core_out, core_in, home_out, home_in, own_out, own_in,
-    fresh_sem, tab_sem, part_send, part_recv, pair_send, pair_recv, pair_local, tail_send, tail_recv,
+    small_sem, fresh_sem, tab_sem, part_send, part_recv, pair_send, pair_recv, pair_local, tail_send, tail_recv,
 ):
     near = (near0, near1, near2, near3, near4)
     chan = lax.axis_index("chan")
     win = lax.axis_index("win")
-    chans = quality.shape[0]
+    chans = spectra.shape[0]
     subs = spectra.shape[1]
     slots = pairs.shape[1]
     rows = 3 * slots
+    pitch = rows + 8
     core = lax.rem(win, 2)
     x_hi = win // 2
     has_left = (chan > 0).astype(jnp.int32)
@@ -85,6 +87,12 @@
     greet((chan, win_across))
     greet((chan, win_cross))
 
+    small = [
+        pltpu.make_async_copy(src, dst, small_sem.at[i])
+        for i, (src, dst) in enumerate(((quality_in, quality), (pairs_out, pairs)))
+    ]
+    for copy in small:
+        copy.start()
     fetched = []
     for group in range(GROUPS):
         copy = pltpu.make_async_copy(
@@ -119,7 +127,7 @@
             real = loose[pl.ds(0, count, stride=2), :]
             imag = loose[pl.ds(1, count, stride=2), :]
             magnitude = jnp.sqrt(real * real + imag * imag)
-            level = jnp.dot(magnitude.astype(jnp.bfloat16), mean_of[...], preferred_element_type=jnp.float32)
+            level = jnp.dot(magnitude.astype(jnp.bfloat16), mean_of, preferred_element_type=jnp.float32)
             weight = 1.0 / (level + tiny_level)
             real = (real * weight).reshape(step, subs, RUNS, LANES)
             imag = (imag * weight).reshape(step, subs, RUNS, LANES)
@@ -145,16 +153,23 @@
         def _():
             to_left.start()
 
-    def both_waits(to_right, to_left):
+    def both_land(to_right, to_left):
+        @pl.when(chan > 0)
+        def _():
+            to_right.wait_recv()
+
         @pl.when(chan < chan_total - 1)
         def _():
+            to_left.wait_recv()
+
+    def both_sent(to_right, to_left):
+        @pl.when(chan < chan_total - 1)
+        def _():
             to_right.wait_send()
-            to_left.wait_recv()
 
         @pl.when(chan > 0)
         def _():
             to_left.wait_send()
-            to_right.wait_recv()
 
     def beside(src, dsts, send, recv):
         return [
@@ -165,6 +180,9 @@
             for side, peer in ((0, chan + 1), (1, chan - 1))
         ]
 
+    mean_of = band_mean()
+    for copy in small:
+        copy.wait()
     whiten(0)
     pl.semaphore_wait(barrier, 3 + 2 * has_left + 2 * has_right)
 
@@ -192,7 +210,7 @@
             copy.start()
             tables.append(copy)
 
-    both_waits(*pair_copies)
+    both_land(*pair_copies)
     local = pltpu.make_async_copy(pair_in, pair_near, pair_local)
     local.start()
     local.wait()
@@ -225,7 +243,7 @@
         runs = PARTS[part][2]
         half = subs * runs
         here = near[part]
-        unroll = 4
+        unroll = 16
 
         def fold(values):
             values = values.astype(jnp.float32).reshape(half // 8, 8, LANES).sum(axis=0)
@@ -240,13 +258,13 @@
                 b = here[rcv_at[p]]
                 real = a[:half] * b[:half] + a[half:] * b[half:]
                 imag = a[half:] * b[:half] - a[:half] * b[half:]
-                cross[pl.ds(p, runs, stride=2 * rows), :] = fold(real)
-                cross[pl.ds(p + rows, runs, stride=2 * rows), :] = fold(imag)
+                cross[pl.ds(p, runs, stride=pitch), :] = fold(real)
+                cross[pl.ds(p + RUNS * pitch, runs, stride=pitch), :] = fold(imag)
             return carry
 
         lax.fori_loop(0, (high - low) // unroll, some, 0)
         for k in range(2 * runs):
-            left_rows[low:high, k * LANES : (k + 1) * LANES] = cross[k * rows + low : k * rows + high, :].astype(
+            left_rows[low:high, k * LANES : (k + 1) * LANES] = cross[((k % 2) * RUNS + k // 2) * pitch + low : ((k % 2) * RUNS + k // 2) * pitch + high, :].astype(
                 jnp.bfloat16
             )
 
@@ -262,7 +280,7 @@
         copy.wait()
 
     for part in range(len(PARTS) - 1):
-        both_waits(*part_copies[part])
+        both_land(*part_copies[part])
         products(part, 0, rows)
         for g in range(WINS):
             total = lags(part, 0, rows, g)
@@ -275,43 +293,86 @@
         )
 
     part = len(PARTS) - 1
-    both_waits(*part_copies[part])
-    products(part, slots, rows)
-    core_copies = []
-    for g in range(2):
-        core_out[g] = (lags(part, slots, rows, g) + sums[g, slots:rows]).astype(jnp.bfloat16)
-        copy = remote(core_out.at[g], core_in.at[g], g, (chan, win_mate))
+    both_land(*part_copies[part])
+    sides = ((0, 2 * slots), (1, slots))
+
+    def to_mate(side, low):
+        for g in range(2):
+            core_out[side, g] = (lags(part, low, low + slots, g) + sums[g, low : low + slots]).astype(jnp.bfloat16)
+        copy = remote(core_out.at[side], core_in.at[side], side, (chan, win_mate))
         copy.start()
-        core_copies.append(copy)
-    home_copies = []
-    ahead = [lags(part, slots, rows, 2 + g) + sums[2 + g, slots:rows] for g in range(2)]
-    for g, to_win in ((0, win_across), (1, win)):
-        core_copies[g].wait()
-        home_out[g] = (ahead[g] + core_in[g].astype(jnp.float32)).astype(jnp.bfloat16)
-        copies = [
-            remote(home_out.at[g, pl.ds(slots, slots)], home_in.at[0, g], 2 + 2 * g, (chan + 1, to_win)),
-            remote(home_out.at[g, pl.ds(0, slots)], home_in.at[1, g], 3 + 2 * g, (chan - 1, to_win)),
-        ]
-        both_ways(*copies)
-        home_copies.append(copies)
+        return copy
+
+    def to_home(side, ahead, core_copy):
+        core_copy.wait_recv()
+        copies = []
+        for g, to_win in ((0, win_across), (1, win)):
+            home_out[side, g] = (ahead[g] + core_in[side, g].astype(jnp.float32)).astype(jnp.bfloat16)
+            copies.append(
+                remote(home_out.at[side, g], home_in.at[side, g], 2 + 2 * side + g, (chan + 1 - 2 * side, to_win))
+            )
+
+        @pl.when(chan < chan_total - 1 if side == 0 else chan > 0)
+        def _():
+            for copy in copies:
+                copy.start()
+
+        return copies
+
+    def kept(low, g):
+        return lags(part, low, low + slots, g) + sums[g, low : low + slots]
+
+    (_, right_low), (_, left_low) = sides
+    products(part, right_low, right_low + slots)
+    core_right = to_mate(0, right_low)
+    ahead = [kept(right_low, 2), kept(right_low, 3)]
+    products(part, left_low, left_low + slots)
+    home_right = to_home(0, ahead, core_right)
+    core_left = to_mate(1, left_low)
+    ahead = [kept(left_low, 2), kept(left_low, 3)]
 
     products(part, 0, slots)
+    home_left = to_home(1, ahead, core_left)
     own_copies = []
-    for g, to_win in ((0, win_cross), (1, win_mate), (2, win_across)):
-        own_out[g] = (lags(part, 0, slots, g) + sums[g, 0:slots]).astype(jnp.bfloat16)
+    for g, to_win in ((0, win_cross), (2, win_across), (1, win_mate)):
+        own_out[g] = kept(0, g).astype(jnp.bfloat16)
         copy = remote(own_out.at[g], own_in.at[g], 6 + g, (chan, to_win))
         copy.start()
         own_copies.append(copy)
-    total = lags(part, 0, slots, 3) + sums[3, 0:slots]
+    total = kept(0, 3)
+
+    for copies in part_copies:
+        both_sent(*copies)
+    both_sent(*pair_copies)
+    core_right.wait_send()
+    core_left.wait_send()
     for copy in own_copies:
         copy.wait()
     for g in range(3):
         total = total + own_in[g].astype(jnp.float32)
-    for copies in home_copies:
-        both_waits(*copies)
+    for to_left in home_left:
+        @pl.when(chan < chan_total - 1)
+        def _():
+            to_left.wait_recv()
+
+        @pl.when(chan > 0)
+        def _():
+            to_left.wait_send()
+
     for g in range(2):
-        total = total + home_in[0, g].astype(jnp.float32) + home_in[1, g].astype(jnp.float32)
-    out[...] = total * (1.0 / math.sqrt(subs * WINS))
+        total = total + home_in[1, g].astype(jnp.float32)
+    for to_right in home_right:
+        @pl.when(chan < chan_total - 1)
+        def _():
+            to_right.wait_send()
+
+        @pl.when(chan > 0)
+        def _():
+            to_right.wait_recv()
+
+    for g in range(2):
+        total = total + home_in[0, g].astype(jnp.float32)
+    out[...] = total
 
 
 def on_device(chan_total, spectra, pair_list, quality):
@@ -322,41 +383,42 @@
     tiles = spectra.reshape(chans, subs, 2, runs, LANES).transpose(0, 1, 3, 2, 4)
     tiles = tiles.reshape(chans, subs, 2 * runs, LANES)
     pairs = pair_list.T
-    vmem = pl.BlockSpec(memory_space=pltpu.VMEM)
-    smem = pl.BlockSpec(memory_space=pltpu.SMEM)
-    anywhere = pl.BlockSpec(memory_space=pl.ANY)
+    hbm = pl.BlockSpec(memory_space=pltpu.HBM)
     sem = pltpu.SemaphoreType.DMA
     bf16 = jnp.bfloat16
-    return pl.pallas_call(
+    total = pl.pallas_call(
         functools.partial(kernel, chan_total),
-        out_shape=jax.ShapeDtypeStruct((slots, WIDE), jnp.float32),
-        in_specs=[smem, smem, vmem, vmem, anywhere, anywhere],
-        out_specs=vmem,
+        out_shape=pltpu.VMEM((slots, WIDE), jnp.float32),
+        in_specs=[hbm] * 4,
+        out_specs=pl.BlockSpec(memory_space=pltpu.VMEM),
         scratch_shapes=[pltpu.VMEM((3 * chans + 1, 2 * subs * part[2], LANES), bf16) for part in PARTS]
         + [
             pltpu.VMEM((GROUPS, chans, subs, 2 * RUNS, LANES), bf16),
             pltpu.VMEM((4 * subs * RUNS * 2, LANES), jnp.float32),
-            pltpu.VMEM((2 * RUNS * rows, LANES), jnp.float32),
+            pltpu.VMEM((2 * RUNS * (rows + 8), LANES), jnp.float32),
             pltpu.VMEM((rows, 2 * RUNS * LANES), bf16),
             pltpu.VMEM((WINS, rows, WIDE), jnp.float32),
             pltpu.VMEM((GROUPS, WINS, 2 * RUNS * LANES, WIDE), bf16),
+            pltpu.SMEM(quality.shape, jnp.int32),
+            pltpu.SMEM(pairs.shape, jnp.int32),
             pltpu.VMEM((2,) + pairs.shape, jnp.int32),
             pltpu.SMEM((2,) + pairs.shape, jnp.int32),
             pltpu.SMEM((rows,), jnp.int32),
             pltpu.SMEM((rows,), jnp.int32),
-            pltpu.VMEM((2, 2 * slots, WIDE), bf16),
-            pltpu.VMEM((2, 2 * slots, WIDE), bf16),
-            pltpu.VMEM((2, 2 * slots, WIDE), bf16),
+            pltpu.VMEM((2, 2, slots, WIDE), bf16),
+            pltpu.VMEM((2, 2, slots, WIDE), bf16),
+            pltpu.VMEM((2, 2, slots, WIDE), bf16),
             pltpu.VMEM((2, 2, slots, WIDE), bf16),
             pltpu.VMEM((3, slots, WIDE), bf16),
             pltpu.VMEM((3, slots, WIDE), bf16),
-            sem((GROUPS,)), sem((GROUPS, WINS)), sem((len(PARTS), 2)), sem((len(PARTS), 2)),
+            sem((2,)), sem((GROUPS,)), sem((GROUPS, WINS)), sem((len(PARTS), 2)), sem((len(PARTS), 2)),
             sem((2,)), sem((2,)), sem, sem((9,)), sem((9,)),
         ],
         compiler_params=pltpu.CompilerParams(
-            collective_id=0, has_side_effects=True, vmem_limit_bytes=56 * 1024 * 1024
+            collective_id=0, has_side_effects=True, vmem_limit_bytes=63 * 1024 * 1024
         ),
-    )(quality, pairs, pairs, jnp.asarray(band_mean()), tiles, jnp.asarray(lag_tables()))
+    )(quality, pairs, tiles, jnp.asarray(lag_tables()))
+    return total * (1.0 / math.sqrt(subs * WINS))
 
 
 def solution(mesh):

time: 74 us -> 71.2 us (0.962)
  Pallas kernels: 72.3 us -> 70.4 us
  local copies, waits for them, and re-layouts: 1.54 us -> 0 us
    pallas_call x1, Pallas kernels: 72.3 us -> 70.4 us  [on_device(): pl.pallas_call(functools.partial(kernel, chan_total), out_shape=pltpu.VME...]
    unnamed x1 -> x0, local copies, waits for them, and re-layouts: 1.54 us -> none
where the time goes in v3:
time: 71.2 us; the launch traced here: 71 us
  Pallas kernels  70.4 us (99%)
    pallas_call x1, Pallas kernels, on_device(): pl.pallas_call(functools.partial(kernel, chan_total), out_shape=pltpu.VME...  70.4 us

profile of v3, /device:TPU:57, one launch (start us, length us, event | category | flops | bytes accessed | tf_op | source)
XLA Modules:
  0.0 71.0 jit_solution(10832260500249778380)
XLA Ops:
  0.0 70.4 %shard_map.46 = f32[96,256]{1,0:T(8,128)S(1)} custom-call(s32[32]{0:T(128)} %quality_in.1, s32[3,96]{1,0:T(4,128)} %bitcast.7, bf16[32,4,64,128]{3,2,1,0:T(8,128)(2,1)} %bitcast.6, bf16[4,4,2048,256]{3,2,1,0:T(8,128)(2,1)} %constant.4.clone.table), custom_call_target="tpu_custom_call" | custom-call | tf_op jit(solution)/shard_map/pallas_call | solution.py:389
  70.4 0.6 broadcast_multiply_fusion

commit v4 on v3

--- a/solution.py
+++ b/solution.py
@@ -19,7 +19,10 @@
 
 RUNS = 8
 GROUPS = NF // (RUNS * LANES)
-PARTS = ((0, 0, 8), (1, 0, 8), (2, 0, 8), (3, 0, 4), (3, 4, 4))
+PARTS = ((0, 0, 8), (1, 0, 8), (2, 0, 8), (3, 0, 4), (3, 4, 2), (3, 6, 2))
+LAST, EXTRA = 4, 5
+TO_RIGHT = (0, 1, 2, EXTRA, 3, LAST)
+TO_LEFT = (0, 1, 2, 3, LAST, EXTRA)
 WINS = 4
 WIDE = LAGS // WINS
 
@@ -47,12 +50,12 @@
 def kernel(
     chan_total, quality_in, pairs_out, spectra, table,
     out,
-    near0, near1, near2, near3, near4, fresh, loose, cross, left_rows, sums, tab,
-    quality, pairs, pair_in, pair_near, src_at, rcv_at,
+    near0, near1, near2, near3, near4, near5, beyond, fresh, loose, cross, left_rows, sums, tab,
+    quality, pairs, pair_in, pair_near, src_at, rcv_at, far_src_at, far_rcv_at, beyond_at,
     core_out, core_in, home_out, home_in, own_out, own_in,
-    small_sem, fresh_sem, tab_sem, part_send, part_recv, pair_send, pair_recv, pair_local, tail_send, tail_recv,
+    small_sem, fresh_sem, tab_sem, part_send, part_recv, far_send, far_recv, pair_send, pair_recv, pair_local, tail_send, tail_recv,
 ):
-    near = (near0, near1, near2, near3, near4)
+    near = (near0, near1, near2, near3, near4, near5)
     chan = lax.axis_index("chan")
     win = lax.axis_index("win")
     chans = spectra.shape[0]
@@ -73,15 +76,15 @@
     def greet(peer):
         pl.semaphore_signal(barrier, inc=1, device_id=peer, device_id_type=MESH)
 
+    @pl.when(chan < chan_total - 1)
+    def _():
+        greet((chan + 1, win))
+        greet((chan + 1, win_across))
+
     @pl.when(chan > 0)
     def _():
         greet((chan - 1, win))
         greet((chan - 1, win_across))
-
-    @pl.when(chan < chan_total - 1)
-    def _():
-        greet((chan + 1, win))
-        greet((chan + 1, win_across))
 
     greet((chan, win_mate))
     greet((chan, win_across))
@@ -93,13 +96,19 @@
     ]
     for copy in small:
         copy.start()
+    halves = [(0, chans // 2), (chans // 2, chans)]
     fetched = []
     for group in range(GROUPS):
-        copy = pltpu.make_async_copy(
-            spectra.at[:, :, pl.ds(group * 2 * RUNS, 2 * RUNS), :], fresh.at[group], fresh_sem.at[group]
-        )
-        copy.start()
-        fetched.append(copy)
+        pieces = halves if group == 0 else [(0, chans)]
+        copies = []
+        for n, (low, high) in enumerate(pieces):
+            copy = pltpu.make_async_copy(
+                spectra.at[pl.ds(low, high - low), :, pl.ds(group * 2 * RUNS, 2 * RUNS), :],
+                fresh.at[group, pl.ds(low, high - low)], fresh_sem.at[group, n],
+            )
+            copy.start()
+            copies.append(copy)
+        fetched.append(copies)
     @pl.when(chan == 0)
     def _():
         for part in range(len(PARTS)):
@@ -107,6 +116,12 @@
         pair_in[0] = jnp.zeros(pair_in.shape[1:], jnp.int32)
         home_in[0] = jnp.zeros(home_in.shape[1:], jnp.bfloat16)
 
+    beyond[chans] = jnp.zeros(beyond.shape[1:], jnp.bfloat16)
+
+    @pl.when(chan < 2)
+    def _():
+        beyond[0:chans] = jnp.zeros((chans,) + beyond.shape[1:], jnp.bfloat16)
+
     @pl.when(chan == chan_total - 1)
     def _():
         for part in range(len(PARTS)):
@@ -114,16 +129,14 @@
         pair_in[1] = jnp.zeros(pair_in.shape[1:], jnp.int32)
         home_in[1] = jnp.zeros(home_in.shape[1:], jnp.bfloat16)
 
-    def whiten(group):
+    def whiten(group, low, high):
         step = 4
         mine = [(p, first, runs) for p, (g, first, runs) in enumerate(PARTS) if g == group]
-        fetched[group].wait()
-
         def some(i, carry):
-            start = i * step
+            start = low + i * step
             block = fresh[group, pl.ds(start, step)]
             count = step * subs * RUNS
-            loose[...] = block.astype(jnp.float32).reshape(2 * count, LANES)
+            loose[0 : 2 * count] = block.astype(jnp.float32).reshape(2 * count, LANES)
             real = loose[pl.ds(0, count, stride=2), :]
             imag = loose[pl.ds(1, count, stride=2), :]
             magnitude = jnp.sqrt(real * real + imag * imag)
@@ -134,13 +147,14 @@
             for j in range(step):
                 good = quality[start + j].astype(jnp.float32)
                 for p, first, runs in mine:
-                    half = subs * runs
-                    for k, values in ((0, real), (1, imag)):
-                        kept = (values[j, :, first : first + runs] * good).reshape(half, LANES)
-                        near[p][chans + start + j, k * half : (k + 1) * half, :] = kept.astype(jnp.bfloat16)
+                    kept = [
+                        (values[j, :, first : first + runs] * good).reshape(subs * runs, LANES)
+                        for values in (real, imag)
+                    ]
+                    near[p][chans + start + j] = jnp.concatenate(kept, axis=0).astype(jnp.bfloat16)
             return carry
 
-        lax.fori_loop(0, chans // step, some, 0)
+        lax.fori_loop(0, (high - low) // step, some, 0)
         for p, first, runs in mine:
             near[p][3 * chans] = jnp.zeros(near[p].shape[1:], jnp.bfloat16)
 
@@ -183,26 +197,36 @@
     mean_of = band_mean()
     for copy in small:
         copy.wait()
-    whiten(0)
+    fetched[0][0].wait()
+    whiten(0, *halves[0])
     pl.semaphore_wait(barrier, 3 + 2 * has_left + 2 * has_right)
 
     pair_copies = beside(pairs_out, [pair_in.at[0], pair_in.at[1]], pair_send, pair_recv)
-    part_copies = []
+    def block_of(p, low, high, sems):
+        count = high - low
+        return beside(
+            near[p].at[pl.ds(chans + low, count)],
+            [near[p].at[pl.ds(low, count)], near[p].at[pl.ds(2 * chans + low, count)]],
+            part_send.at[sems], part_recv.at[sems],
+        )
+
+    part_copies = [block_of(p, 0, chans, p) for p in range(1, len(PARTS))]
+    part_copies.insert(0, block_of(0, *halves[1], 0))
+    first_copies = block_of(0, *halves[0], len(PARTS))
+    both_ways(*first_copies)
     for group in range(GROUPS):
-        if group > 0:
-            whiten(group)
-        for p, (g, first, runs) in enumerate(PARTS):
-            if g == group:
-                copies = beside(
-                    near[p].at[pl.ds(chans, chans)],
-                    [near[p].at[pl.ds(0, chans)], near[p].at[pl.ds(2 * chans, chans)]],
-                    part_send.at[p], part_recv.at[p],
-                )
-                both_ways(*copies)
-                part_copies.append(copies)
+        fetched[group][-1].wait()
+        whiten(group, *(halves[1] if group == 0 else (0, chans)))
+        rightward = [p for p in TO_RIGHT if PARTS[p][0] == group]
+        leftward = [p for p in TO_LEFT if PARTS[p][0] == group]
+        for p, q in zip(rightward, leftward):
+            both_ways(part_copies[p][0], part_copies[q][1])
         if group == 0:
             both_ways(*pair_copies)
-
+    pass_on = pltpu.make_async_remote_copy(
+        src_ref=near[EXTRA].at[pl.ds(0, chans)], dst_ref=beyond.at[pl.ds(0, chans)],
+        send_sem=far_send, recv_sem=far_recv, device_id=(chan + 1, win), device_id_type=MESH,
+    )
     tables = []
     for group in range(GROUPS):
         for g, quarter in enumerate((win_cross, win_mate, win_across, win)):
@@ -226,6 +250,11 @@
             rcv_at[row] = jnp.where(fits, at, empty)
 
         put(p, pairs[0, p], pairs[1, p], pairs[2, p], 0, 3 * chans)
+        at = pairs[1, p] - base
+        fits = (pairs[2, p] != 0) & (at >= -chans) & (at < 3 * chans)
+        far_src_at[p] = jnp.where(fits, pairs[0, p] - base, empty)
+        far_rcv_at[p] = jnp.where(fits & (at >= 0), at, empty)
+        beyond_at[p] = jnp.where(fits & (at < 0), at + chans, chans)
         between = has_left * has_right
         put(
             slots + p, pair_near[0, 0, p], pair_near[0, 1, p], pair_near[0, 2, p] * between,
@@ -239,23 +268,28 @@
 
     lax.fori_loop(0, slots, place, 0)
 
-    def products(part, low, high):
+    def products(part, low, high, column=0, sources=src_at, receivers=rcv_at, further=None):
         runs = PARTS[part][2]
         half = subs * runs
         here = near[part]
         unroll = 16
+        kind = jnp.bfloat16 if half >= 16 else jnp.float32
 
         def fold(values):
             values = values.astype(jnp.float32).reshape(half // 8, 8, LANES).sum(axis=0)
-            if runs == 4:
-                values = values[:4] + values[4:]
+            count = 8
+            while count > runs:
+                count //= 2
+                values = values[:count] + values[count:]
             return values
 
         def some(i, carry):
             for j in range(unroll):
                 p = low + i * unroll + j
-                a = here[src_at[p]]
-                b = here[rcv_at[p]]
+                a = here[sources[p]].astype(kind)
+                b = here[receivers[p]].astype(kind)
+                if further is not None:
+                    b = b + beyond[further[p]].astype(kind)
                 real = a[:half] * b[:half] + a[half:] * b[half:]
                 imag = a[half:] * b[:half] - a[:half] * b[half:]
                 cross[pl.ds(p, runs, stride=pitch), :] = fold(real)
@@ -264,12 +298,12 @@
 
         lax.fori_loop(0, (high - low) // unroll, some, 0)
         for k in range(2 * runs):
-            left_rows[low:high, k * LANES : (k + 1) * LANES] = cross[((k % 2) * RUNS + k // 2) * pitch + low : ((k % 2) * RUNS + k // 2) * pitch + high, :].astype(
-                jnp.bfloat16
-            )
-
-    def lags(part, low, high, g):
-        group, first, runs = PARTS[part]
+            start = ((k % 2) * RUNS + k // 2) * pitch
+            left_rows[low:high, column + k * LANES : column + (k + 1) * LANES] = cross[
+                start + low : start + high, :
+            ].astype(jnp.bfloat16)
+
+    def lags(low, high, g, group, first, runs):
         depth = 2 * runs * LANES
         return jnp.dot(
             left_rows[low:high, :depth], tab[group, g, 2 * first * LANES : 2 * first * LANES + depth, :],
@@ -279,11 +313,21 @@
     for copy in tables:
         copy.wait()
 
-    for part in range(len(PARTS) - 1):
+    both_land(*first_copies)
+    for part in range(LAST):
         both_land(*part_copies[part])
+        if part == LAST - 1:
+            @pl.when(chan > 0)
+            def _():
+                part_copies[EXTRA][0].wait_recv()
+
+            @pl.when((chan > 0) & (chan < chan_total - 1))
+            def _():
+                pass_on.start()
+
         products(part, 0, rows)
         for g in range(WINS):
-            total = lags(part, 0, rows, g)
+            total = lags(0, rows, g, *PARTS[part])
             sums[g] = total if part == 0 else total + sums[g]
 
     def remote(src, dst, which, peer):
@@ -292,13 +336,15 @@
             device_id=peer, device_id_type=MESH,
         )
 
-    part = len(PARTS) - 1
-    both_land(*part_copies[part])
+    both_land(*part_copies[LAST])
     sides = ((0, 2 * slots), (1, slots))
 
-    def to_mate(side, low):
+    def kept(low, g, runs):
+        return lags(low, low + slots, g, *PARTS[LAST][:2], runs) + sums[g, low : low + slots]
+
+    def to_mate(side, low, runs):
         for g in range(2):
-            core_out[side, g] = (lags(part, low, low + slots, g) + sums[g, low : low + slots]).astype(jnp.bfloat16)
+            core_out[side, g] = kept(low, g, runs).astype(jnp.bfloat16)
         copy = remote(core_out.at[side], core_in.at[side], side, (chan, win_mate))
         copy.start()
         return copy
@@ -319,31 +365,49 @@
 
         return copies
 
-    def kept(low, g):
-        return lags(part, low, low + slots, g) + sums[g, low : low + slots]
-
     (_, right_low), (_, left_low) = sides
-    products(part, right_low, right_low + slots)
-    core_right = to_mate(0, right_low)
-    ahead = [kept(right_low, 2), kept(right_low, 3)]
-    products(part, left_low, left_low + slots)
+    alone = PARTS[LAST][2]
+    whole = alone + PARTS[EXTRA][2]
+    extra_column = 2 * alone * LANES
+    products(LAST, right_low, right_low + slots)
+    core_right = to_mate(0, right_low, alone)
+    ahead = [kept(right_low, 2, alone), kept(right_low, 3, alone)]
+    products(LAST, left_low, left_low + slots)
     home_right = to_home(0, ahead, core_right)
-    core_left = to_mate(1, left_low)
-    ahead = [kept(left_low, 2), kept(left_low, 3)]
-
-    products(part, 0, slots)
+
+    @pl.when(chan < chan_total - 1)
+    def _():
+        part_copies[EXTRA][1].wait_recv()
+
+    products(EXTRA, left_low, left_low + slots, extra_column)
+    core_left = to_mate(1, left_low, whole)
+    ahead = [kept(left_low, 2, whole), kept(left_low, 3, whole)]
+
+    products(LAST, 0, slots)
     home_left = to_home(1, ahead, core_left)
+
+    @pl.when(chan >= 2)
+    def _():
+        pass_on.wait_recv()
+
+    products(EXTRA, 0, slots, extra_column, far_src_at, far_rcv_at, beyond_at)
     own_copies = []
     for g, to_win in ((0, win_cross), (2, win_across), (1, win_mate)):
-        own_out[g] = kept(0, g).astype(jnp.bfloat16)
+        own_out[g] = kept(0, g, whole).astype(jnp.bfloat16)
         copy = remote(own_out.at[g], own_in.at[g], 6 + g, (chan, to_win))
         copy.start()
         own_copies.append(copy)
-    total = kept(0, 3)
+    total = kept(0, 3, whole)
 
     for copies in part_copies:
         both_sent(*copies)
+    both_sent(*first_copies)
     both_sent(*pair_copies)
+
+    @pl.when((chan > 0) & (chan < chan_total - 1))
+    def _():
+        pass_on.wait_send()
+
     core_right.wait_send()
     core_left.wait_send()
     for copy in own_copies:
@@ -391,11 +455,14 @@
         out_shape=pltpu.VMEM((slots, WIDE), jnp.float32),
         in_specs=[hbm] * 4,
         out_specs=pl.BlockSpec(memory_space=pltpu.VMEM),
-        scratch_shapes=[pltpu.VMEM((3 * chans + 1, 2 * subs * part[2], LANES), bf16) for part in PARTS]
+        scratch_shapes=[
+            pltpu.VMEM((3 * chans + 1, 2 * subs * part[2], LANES), bf16) for part in PARTS
+        ]
         + [
+            pltpu.VMEM((chans + 1, 2 * subs * PARTS[EXTRA][2], LANES), bf16),
             pltpu.VMEM((GROUPS, chans, subs, 2 * RUNS, LANES), bf16),
-            pltpu.VMEM((4 * subs * RUNS * 2, LANES), jnp.float32),
-            pltpu.VMEM((2 * RUNS * (rows + 8), LANES), jnp.float32),
+            pltpu.VMEM((4 * subs * RUNS * 2 + 8, LANES), jnp.float32),
+            pltpu.VMEM(((2 * RUNS + 1) * (rows + 8), LANES), jnp.float32),
             pltpu.VMEM((rows, 2 * RUNS * LANES), bf16),
             pltpu.VMEM((WINS, rows, WIDE), jnp.float32),
             pltpu.VMEM((GROUPS, WINS, 2 * RUNS * LANES, WIDE), bf16),
@@ -405,14 +472,17 @@
             pltpu.SMEM((2,) + pairs.shape, jnp.int32),
             pltpu.SMEM((rows,), jnp.int32),
             pltpu.SMEM((rows,), jnp.int32),
+            pltpu.SMEM((slots,), jnp.int32),
+            pltpu.SMEM((slots,), jnp.int32),
+            pltpu.SMEM((slots,), jnp.int32),
             pltpu.VMEM((2, 2, slots, WIDE), bf16),
             pltpu.VMEM((2, 2, slots, WIDE), bf16),
             pltpu.VMEM((2, 2, slots, WIDE), bf16),
             pltpu.VMEM((2, 2, slots, WIDE), bf16),
             pltpu.VMEM((3, slots, WIDE), bf16),
             pltpu.VMEM((3, slots, WIDE), bf16),
-            sem((2,)), sem((GROUPS,)), sem((GROUPS, WINS)), sem((len(PARTS), 2)), sem((len(PARTS), 2)),
-            sem((2,)), sem((2,)), sem, sem((9,)), sem((9,)),
+            sem((2,)), sem((GROUPS, 2)), sem((GROUPS, WINS)), sem((len(PARTS) + 1, 2)), sem((len(PARTS) + 1, 2)),
+            sem, sem, sem((2,)), sem((2,)), sem, sem((9,)), sem((9,)),
         ],
         compiler_params=pltpu.CompilerParams(
             collective_id=0, has_side_effects=True, vmem_limit_bytes=63 * 1024 * 1024

time: 71.2 us -> 70.7 us (level)
  Pallas kernels: 70.4 us -> 69.3 us
    pallas_call x1, Pallas kernels: 70.4 us -> 69.3 us  [on_device(): pl.pallas_call(functools.partial(kernel, chan_total), out_shape=pltpu.VME...]
where the time goes in v4:
time: 70.7 us; the launch traced here: 70 us
  Pallas kernels  69.3 us (98%)
    pallas_call x1, Pallas kernels, on_device(): pl.pallas_call(functools.partial(kernel, chan_total), out_shape=pltpu.VME...  69.3 us

profile of v4, /device:TPU:57, one launch (start us, length us, event | category | flops | bytes accessed | tf_op | source)
XLA Modules:
  0.0 70.0 jit_solution(4101735765895399455)
XLA Ops:
  0.0 69.3 %shard_map.46 = f32[96,256]{1,0:T(8,128)S(1)} custom-call(s32[32]{0:T(128)} %quality_in.1, s32[3,96]{1,0:T(4,128)} %bitcast.7, bf16[32,4,64,128]{3,2,1,0:T(8,128)(2,1)} %bitcast.6, bf16[4,4,2048,256]{3,2,1,0:T(8,128)(2,1)} %constant.4.clone.table), custom_call_target="tpu_custom_call" | custom-call | tf_op jit(solution)/shard_map/pallas_call | solution.py:453
  69.3 0.6 broadcast_multiply_fusion

commit v5 on v4

--- a/solution.py
+++ b/solution.py
@@ -339,28 +339,30 @@
     both_land(*part_copies[LAST])
     sides = ((0, 2 * slots), (1, slots))
 
-    def kept(low, g, runs):
-        return lags(low, low + slots, g, *PARTS[LAST][:2], runs) + sums[g, low : low + slots]
+    def kept(low, g, runs, part=LAST):
+        return lags(low, low + slots, g, *PARTS[part][:2], runs) + sums[g, low : low + slots]
 
     def to_mate(side, low, runs):
+        copies = []
         for g in range(2):
             core_out[side, g] = kept(low, g, runs).astype(jnp.bfloat16)
-        copy = remote(core_out.at[side], core_in.at[side], side, (chan, win_mate))
-        copy.start()
-        return copy
-
-    def to_home(side, ahead, core_copy):
-        core_copy.wait_recv()
+            copy = remote(core_out.at[side, g], core_in.at[side, g], 2 * side + g, (chan, win_mate))
+            copy.start()
+            copies.append(copy)
+        return copies
+
+    def to_home(side, ahead, core_copies):
         copies = []
         for g, to_win in ((0, win_across), (1, win)):
+            core_copies[g].wait_recv()
             home_out[side, g] = (ahead[g] + core_in[side, g].astype(jnp.float32)).astype(jnp.bfloat16)
-            copies.append(
-                remote(home_out.at[side, g], home_in.at[side, g], 2 + 2 * side + g, (chan + 1 - 2 * side, to_win))
+            copy = remote(
+                home_out.at[side, g], home_in.at[side, g], 4 + 2 * side + g, (chan + 1 - 2 * side, to_win)
             )
-
-        @pl.when(chan < chan_total - 1 if side == 0 else chan > 0)
-        def _():
-            for copy in copies:
+            copies.append(copy)
+
+            @pl.when(chan < chan_total - 1 if side == 0 else chan > 0)
+            def _():
                 copy.start()
 
         return copies
@@ -385,19 +387,21 @@
 
     products(LAST, 0, slots)
     home_left = to_home(1, ahead, core_left)
+    for g in range(WINS):
+        sums[g, 0:slots] = kept(0, g, alone)
 
     @pl.when(chan >= 2)
     def _():
         pass_on.wait_recv()
 
-    products(EXTRA, 0, slots, extra_column, far_src_at, far_rcv_at, beyond_at)
+    products(EXTRA, 0, slots, 0, far_src_at, far_rcv_at, beyond_at)
     own_copies = []
     for g, to_win in ((0, win_cross), (2, win_across), (1, win_mate)):
-        own_out[g] = kept(0, g, whole).astype(jnp.bfloat16)
-        copy = remote(own_out.at[g], own_in.at[g], 6 + g, (chan, to_win))
+        own_out[g] = kept(0, g, PARTS[EXTRA][2], EXTRA).astype(jnp.bfloat16)
+        copy = remote(own_out.at[g], own_in.at[g], 8 + g, (chan, to_win))
         copy.start()
         own_copies.append(copy)
-    total = kept(0, 3, whole)
+    total = kept(0, 3, PARTS[EXTRA][2], EXTRA)
 
     for copies in part_copies:
         both_sent(*copies)
@@ -408,8 +412,8 @@
     def _():
         pass_on.wait_send()
 
-    core_right.wait_send()
-    core_left.wait_send()
+    for copy in core_right + core_left:
+        copy.wait_send()
     for copy in own_copies:
         copy.wait()
     for g in range(3):
@@ -482,7 +486,7 @@
             pltpu.VMEM((3, slots, WIDE), bf16),
             pltpu.VMEM((3, slots, WIDE), bf16),
             sem((2,)), sem((GROUPS, 2)), sem((GROUPS, WINS)), sem((len(PARTS) + 1, 2)), sem((len(PARTS) + 1, 2)),
-            sem, sem, sem((2,)), sem((2,)), sem, sem((9,)), sem((9,)),
+            sem, sem, sem((2,)), sem((2,)), sem, sem((11,)), sem((11,)),
         ],
         compiler_params=pltpu.CompilerParams(
             collective_id=0, has_side_effects=True, vmem_limit_bytes=63 * 1024 * 1024

time: 70.7 us -> 71 us (level)
  no operation moved by 1% of the time
where the time goes in v5:
time: 71 us; the launch traced here: 70.4 us
  Pallas kernels  69.7 us (98%)
    pallas_call x1, Pallas kernels, on_device(): pl.pallas_call(functools.partial(kernel, chan_total), out_shape=pltpu.VME...  69.7 us

profile of v5, /device:TPU:57, one launch (start us, length us, event | category | flops | bytes accessed | tf_op | source)
XLA Modules:
  0.0 70.4 jit_solution(5798815463183570683)
XLA Ops:
  0.0 69.7 %shard_map.46 = f32[96,256]{1,0:T(8,128)S(1)} custom-call(s32[32]{0:T(128)} %quality_in.1, s32[3,96]{1,0:T(4,128)} %bitcast.7, bf16[32,4,64,128]{3,2,1,0:T(8,128)(2,1)} %bitcast.6, bf16[4,4,2048,256]{3,2,1,0:T(8,128)(2,1)} %constant.4.clone.table), custom_call_target="tpu_custom_call" | custom-call | tf_op jit(solution)/shard_map/pallas_call | solution.py:457
  69.7 0.6 broadcast_multiply_fusion

commit v6 on v4

--- a/solution.py
+++ b/solution.py
@@ -339,8 +339,8 @@
     both_land(*part_copies[LAST])
     sides = ((0, 2 * slots), (1, slots))
 
-    def kept(low, g, runs):
-        return lags(low, low + slots, g, *PARTS[LAST][:2], runs) + sums[g, low : low + slots]
+    def kept(low, g, runs, part=LAST):
+        return lags(low, low + slots, g, *PARTS[part][:2], runs) + sums[g, low : low + slots]
 
     def to_mate(side, low, runs):
         for g in range(2):
@@ -385,19 +385,21 @@
 
     products(LAST, 0, slots)
     home_left = to_home(1, ahead, core_left)
+    for g in range(WINS):
+        sums[g, 0:slots] = kept(0, g, alone)
 
     @pl.when(chan >= 2)
     def _():
         pass_on.wait_recv()
 
-    products(EXTRA, 0, slots, extra_column, far_src_at, far_rcv_at, beyond_at)
+    products(EXTRA, 0, slots, 0, far_src_at, far_rcv_at, beyond_at)
     own_copies = []
     for g, to_win in ((0, win_cross), (2, win_across), (1, win_mate)):
-        own_out[g] = kept(0, g, whole).astype(jnp.bfloat16)
+        own_out[g] = kept(0, g, PARTS[EXTRA][2], EXTRA).astype(jnp.bfloat16)
         copy = remote(own_out.at[g], own_in.at[g], 6 + g, (chan, to_win))
         copy.start()
         own_copies.append(copy)
-    total = kept(0, 3, whole)
+    total = kept(0, 3, PARTS[EXTRA][2], EXTRA)
 
     for copies in part_copies:
         both_sent(*copies)

time: 70.7 us -> 70.7 us (level)
  no operation moved by 1% of the time
where the time goes in v6:
time: 70.7 us; the launch traced here: 70 us
  Pallas kernels  69.3 us (98%)
    pallas_call x1, Pallas kernels, on_device(): pl.pallas_call(functools.partial(kernel, chan_total), out_shape=pltpu.VME...  69.3 us

profile of v6, /device:TPU:57, one launch (start us, length us, event | category | flops | bytes accessed | tf_op | source)
XLA Modules:
  0.0 70.0 jit_solution(14934433979687212670)
XLA Ops:
  0.0 69.3 %shard_map.46 = f32[96,256]{1,0:T(8,128)S(1)} custom-call(s32[32]{0:T(128)} %quality_in.1, s32[3,96]{1,0:T(4,128)} %bitcast.7, bf16[32,4,64,128]{3,2,1,0:T(8,128)(2,1)} %bitcast.6, bf16[4,4,2048,256]{3,2,1,0:T(8,128)(2,1)} %constant.4.clone.table), custom_call_target="tpu_custom_call" | custom-call | tf_op jit(solution)/shard_map/pallas_call | solution.py:455
  69.3 0.6 broadcast_multiply_fusion
